TPU v7x, 32 devices: a whole 2x2x4 slice. The times are simulated.
32 devices in a mesh: groups: 2 (over x), seg: 16 (over z, y, core).
Axes of the slice: x: 2, y: 2, z: 4, core: 2. Of those that a mesh axis runs over, the one named last changes fastest.
Arguments:
- psi_start: float32 [32, 1, 256, 256], P(('groups', 'seg')), parts along dimension 0, may hold values from -400 to 400
- block_sizes: int32 [32, 1, 2], P(('groups', 'seg')), parts along dimension 0, may hold values from 42 to 256, as said below
- environment: bfloat16 [32, 2, 1, 34, 256, 256], P(('groups', 'seg')), parts along dimension 0, may hold values from -3 to 3, as said below
Outputs:
- wavefunction: float32 [32, 1, 256, 256], P(('groups', 'seg')), parts along dimension 0
- energies: float32 [32, 2], P(('groups', 'seg')), parts along dimension 0
- sweep_energy: float32 [4], P('groups'), parts along dimension 0
There are 2 independent parts, one for each index of `groups`. A program takes and returns all parts, laid end to end along the dimension named above; each array names one. Nothing has to cross between parts.
Inputs may be any that keep to these rules, and one draw needn't show every extreme that they name: `block_sizes`: live left and right states of a sector block; in every draw some block has 256 of both. Every matrix environment[d, e, s, k] is symmetric.
All inputs are finite; a program needn't handle non-finite values.
Results may differ from a plain program's by a relative error of at most 0.0045.
Values may be sent and summed in bfloat16 or wider, within the bound.
A program may use at most 128 MiB of HBM per device.

v0:
```python
import jax
import jax.numpy as jnp
from jax import lax
from jax.sharding import PartitionSpec as P

ITERS = 2


EPSILON = 1e-06
PRECISE = lax.Precision.HIGHEST


def swapped(shard, axis, stride):
    return lax.ppermute(shard, axis, [(i, i ^ 1 << stride) for i in range(lax.axis_size(axis))])


def in_frame(state_field, flipped):
    return jnp.where(flipped[:, None, None, None], jnp.swapaxes(state_field, -1, -2), state_field)


def block_mask(block_dims, flipped, edge_size):
    first_live = jnp.where(flipped[:, None], block_dims[..., 1], block_dims[..., 0])
    second_live = jnp.where(flipped[:, None], block_dims[..., 0], block_dims[..., 1])
    positions = lax.iota(jnp.int32, edge_size)
    row_live = positions[None, None, :, None] < first_live[..., None, None]
    col_live = positions[None, None, None, :] < second_live[..., None, None]
    return (row_live & col_live).astype(jnp.float32)


def apply_operator(state_field, own_env, other_env, live_mask):
    lowered = state_field.astype(jnp.bfloat16)
    half_products = jnp.einsum(
        "nskij,nsjl->nskil", own_env, lowered, preferred_element_type=jnp.float32
    ).astype(jnp.bfloat16)
    result = jnp.einsum(
        "nskil,nsklm->nsim", half_products, other_env, preferred_element_type=jnp.float32
    )
    return result * live_mask


def diagonal_terms(own_env, other_env):
    own_diag = jnp.diagonal(own_env, axis1=-2, axis2=-1).astype(jnp.float32)
    other_diag = jnp.diagonal(other_env, axis1=-2, axis2=-1).astype(jnp.float32)
    return jnp.einsum("nski,nskj->nsij", own_diag, other_diag, precision=PRECISE)


def ritz_pair(rayleigh, coupling, curvature):
    half_gap = 0.5 * (rayleigh - curvature)
    energy_now = 0.5 * (rayleigh + curvature) - jnp.sqrt(half_gap * half_gap + coupling * coupling)
    weight_old = curvature - energy_now
    weight_new = -coupling
    length_pair = jnp.sqrt(weight_old * weight_old + weight_new * weight_new)
    return (energy_now, weight_old / length_pair, weight_new / length_pair)


def refine(
    initial,
    own_env,
    other_env,
    live_mask,
    precondition,
    total_start,
    total_rayleigh,
    orthogonal,
    total_coupling,
):
    vector = initial * live_mask
    norm_total = total_start(jnp.sum(vector * vector))
    vector = vector / jnp.sqrt(norm_total + EPSILON)
    image = apply_operator(vector, own_env, other_env, live_mask)
    energy_list = []
    for iteration in range(ITERS):
        rayleigh = total_rayleigh(jnp.sum(vector * image))
        correction = (image - rayleigh * vector) / jnp.maximum(
            jnp.abs(precondition - rayleigh), 1.0
        )
        correction = orthogonal(vector, correction)
        corr_image = apply_operator(correction, own_env, other_env, live_mask)
        pair_sums = total_coupling(
            jnp.stack([jnp.sum(vector * corr_image), jnp.sum(correction * corr_image)])
        )
        energy_now, weight_old, weight_new = ritz_pair(rayleigh, pair_sums[0], pair_sums[1])
        vector = weight_old * vector + weight_new * correction
        image = weight_old * image + weight_new * corr_image
        energy_list.append(energy_now)
    return (vector, jnp.stack(energy_list))


def per_device(psi_start, block_sizes, environment):
    seg_index = lax.axis_index("seg")
    odd_device = seg_index % 2 == 1
    edge_size = psi_start.shape[-1]
    own_env = environment[:, 0]
    other_env = swapped(environment[:, 1], "seg", 0)
    flipped = odd_device[None]

    def total_start(local_part):
        return local_part + swapped(local_part, "seg", 0)

    def total_rayleigh(local_part):
        return local_part + swapped(local_part, "seg", 0)

    def orthogonal(vector, correction):
        local_part = jnp.sum(vector * correction)
        correlation = local_part + swapped(local_part, "seg", 0)
        correction = correction - correlation * vector
        squared = jnp.sum(correction * correction)
        squared = squared + swapped(squared, "seg", 0)
        return correction / jnp.sqrt(squared + EPSILON)

    def total_coupling(local_part):
        return local_part + swapped(local_part, "seg", 0)

    live_mask = block_mask(block_sizes, flipped, edge_size)
    framed = in_frame(psi_start, flipped)
    precondition = diagonal_terms(own_env, other_env)
    vector, energy_list = refine(
        framed,
        own_env,
        other_env,
        live_mask,
        precondition,
        total_start,
        total_rayleigh,
        orthogonal,
        total_coupling,
    )
    final = in_frame(vector, flipped)[:1] * edge_size
    bonds = lax.axis_size("seg") // 2
    bond_index = (seg_index // 2).astype(jnp.float32)
    bond_weight = 1.0 + 2.0 * bond_index / float(max(bonds - 1, 1))
    contribution = jnp.where(odd_device, 0.0, bond_weight * energy_list / float(bonds))
    sweep_energy = lax.psum(contribution, "seg")
    return (final, energy_list[None], sweep_energy)


def solution(mesh):
    in_specs = (
        P(("groups", "seg"), None, None, None),
        P(("groups", "seg"), None, None),
        P(("groups", "seg"), None, None, None, None, None),
    )
    out_specs = (P(("groups", "seg"), None, None, None), P(("groups", "seg"), None), P("groups"))
    return jax.shard_map(
        per_device, mesh=mesh, in_specs=in_specs, out_specs=out_specs, check_vma=False
    )
```

profile of v0, /device:TPU:0, one launch (start us, length us, event | category | flops | bytes accessed | tf_op | source)
XLA Modules:
  0.0 147.5 jit_solution(13022581633200386854)
XLA Ops:
  0.6 8.1 %fusion.90 = (bf16[1,1,1,34,256,256]{5,4,3,2,1,0:T(8,128)(2,1)}, bf16[1,1,34,256,256]{4,3,2,1,0:T(8,128)(2,1)}) fusion(bf16[1,2,1,34,256,256]{5,4,3,2,1,0:T(8,128)(2,1)} %param.5), kind=kLoop, calls=%fused_computation.76 | loop fusion | bytes 17825792 | tf_op jit(solution)/shard_map/slice | solution.py:93
  9.2 0.6 fusion.93
  12.6 0.7 multiply_reduce_fusion.6
  13.4 15.4 %copy.15 = bf16[1,1,1,34,256,256]{3,5,4,2,1,0:T(8,128)(2,1)} copy(bf16[1,1,1,34,256,256]{5,4,3,2,1,0:T(8,128)(2,1)} %get-tuple-element.13) | data formatting | bytes 8912896
  28.7 2.7 %gather_fusion = bf16[256,34]{1,0:T(8,128)(2,1)S(1)} fusion(bf16[34,256,256]{0,2,1:T(8,128)(2,1)} %bitcast.189, s32[256]{0:T(256)S(1)} %bitcast.187), kind=kCustom, calls=%fused_computation | custom fusion | bytes 36864 | tf_op jit(solution)/shard_map/jit(diagonal)/gather | solution.py:42
  32.9 7.9 %fusion.66 = (f32[]{:T(128)}, f32[256,256]{1,0:T(8,128)S(1)}) fusion(f32[1,1,256,256]{3,2,1,0:T(8,128)S(1)} %broadcast_divide_fusion.2, bf16[1,1,34,256,256]{4,3,2,1,0:T(8,128)(2,1)} %collective-permute-done.1, bf16[1,2,1,34,256,256]{5,4,3,2,1,0:T(8,128)(2,1)} %param.5, pred[256]{0:T(512)(128)(4,1)S(1)} %get-tuple-element.25, ...), kind=kOutput, calls=%fused_computation.38 | convolution fusion | flops 2284257280 | bytes 9700356 | tf_op jit(solution)/shard_map/nskil,nsklm->nsim/dot_general | solution.py:35
  40.8 0.5 collective-permute-start.2
  41.3 15.4 %copy.12 = bf16[34,256,256]{0,2,1:T(8,128)(2,1)} copy(bf16[34,256,256]{2,1,0:T(8,128)(2,1)} %bitcast.11) | data formatting | bytes 8912896 | tf_op jit(solution)/shard_map/reshape.13
  56.6 2.7 %gather_fusion.1 = bf16[256,34]{1,0:T(8,128)(2,1)S(1)} fusion(bf16[34,256,256]{0,2,1:T(8,128)(2,1)} %copy.12, s32[256]{0:T(256)S(1)} %bitcast.188), kind=kCustom, calls=%fused_computation.1 | custom fusion | bytes 36864 | tf_op jit(solution)/shard_map/jit(diagonal)/gather | solution.py:43
  60.6 0.8 multiply_reduce_fusion.5
  61.5 1.2 collective-permute-done.3
  64.0 0.7 multiply_reduce_fusion.4
  64.9 1.0 collective-permute-done.4
  67.3 8.0 %fusion.64 = (f32[]{:T(128)}, f32[]{:T(128)}, f32[256,256]{1,0:T(8,128)S(1)}) fusion(f32[1,1,256,256]{3,2,1,0:T(8,128)S(1)} %broadcast_divide_fusion.2, f32[]{:T(128)S(6)} %sqrt.22, f32[1,1,256,256]{3,2,1,0:T(8,128)S(1)} %get-tuple-element.12, f32[]{:T(128)S(6)} %add.86, bf16[1,1,34,256,256]{4,3,2,1,0:T(8,128)(2,1)} %collective-permute-done.1, ...), kind=kOutput, calls=%fused_computation.33 | convolution fusion | flops 2284781568 | bytes 10226696 | tf_op jit(solution)/shard_map/nskil,nsklm->nsim/dot_general | solution.py:35
  75.3 1.4 pad_maximum_fusion
  76.9 0.9 collective-permute-done.5
  77.8 1.4 fusion.109
  79.2 0.6 fusion.92
  83.8 0.7 fusion.63
  84.7 1.2 collective-permute-done.6
  87.1 0.7 multiply_reduce_fusion.3
  88.0 1.2 collective-permute-done.7
  90.4 0.7 multiply_reduce_fusion.2
  91.3 1.2 collective-permute-done.8
  93.8 7.9 %multiply_reduce_fusion.1 = (f32[]{:T(128)}, f32[]{:T(128)}) fusion(f32[1,1,256,256]{3,2,1,0:T(8,128)S(1)} %get-tuple-element.10, f32[]{:T(128)S(6)} %sqrt.25, f32[1,1,256,256]{3,2,1,0:T(8,128)S(1)} %get-tuple-element.8, f32[]{:T(128)S(6)} %add.97, bf16[1,1,34,256,256]{4,3,2,1,0:T(8,128)(2,1)} %collective-permute-done.1, ...), kind=kOutput, calls=%fused_computation.43 | convolution fusion | flops 2284781568 | bytes 9964552 | tf_op jit(solution)/shard_map/nskil,nsklm->nsim/dot_general | solution.py:35
  101.7 1.4 pad_maximum_fusion.1
  103.3 0.9 collective-permute-done.9
  104.2 1.4 fusion.108
  105.6 0.6 fusion.91
  110.2 0.6 fusion.83
  110.9 35.7 %psum.7 = f32[2]{0:T(128)} all-reduce(f32[2]{0:T(128)S(1)} %broadcast_select_fusion), channel_id=1, replica_groups=mesh['groups'=2,'seg'=16] {'seg'}, use_global_device_ids=true, to_apply=%region_11.12 | all-reduce | flops 2 | bytes 16 | tf_op jit(solution)/shard_map/psum | solution.py:133
  146.7 0.7 fusion.62
  (23 shorter events, 2.5 us)
Async XLA Ops:
  0.6 8.6 %copy-start.1 = (s32[1,1,2]{2,1,0:T(1,128)S(1)}, s32[1,1,2]{2,1,0:T(1,128)}, u32[]{:S(2)}) copy-start(s32[1,1,2]{2,1,0:T(1,128)} %param.4) | copy-start | bytes 28
  0.6 11.8 %copy-start = (f32[1,1,256,256]{3,2,1,0:T(8,128)S(1)}, f32[1,1,256,256]{3,2,1,0:T(8,128)}, u32[]{:S(2)}) copy-start(f32[1,1,256,256]{3,2,1,0:T(8,128)} %param.3) | copy-start | bytes 786436
  8.8 24.1 %collective-permute-start.1 = (bf16[1,1,34,256,256]{4,3,2,1,0:T(8,128)(2,1)}, bf16[1,1,34,256,256]{4,3,2,1,0:T(8,128)(2,1)}, u32[]{:S(2)}, u32[]{:S(2)}) collective-permute-start(bf16[1,1,34,256,256]{4,3,2,1,0:T(8,128)(2,1)} %get-tuple-element.14), channel_id=1, source_target_pairs={{0,1},{1,0},{2,3},{3,2},{4,5},{5,4},{6,7},{7,6},{8,9},{9,8},{10,11... | collective-permute-start | bytes 13369352 | tf_op jit(solution)/shard_map/ppermute | solution.py:14
  13.3 18.1 %collective-permute-start = (f32[]{:T(128)}, f32[]{:T(128)}, u32[]{:S(2)}, u32[]{:S(2)}) collective-permute-start(f32[]{:T(128)} %multiply_reduce_fusion.6), channel_id=1, source_target_pairs={{0,1},{1,0},{2,3},{3,2},{4,5},{5,4},{6,7},{7,6},{8,9},{9,8},{10,11... | collective-permute-start | bytes 20 | tf_op jit(solution)/shard_map/ppermute | solution.py:14
  40.8 18.5 %collective-permute-start.2 = (f32[]{:T(128)}, f32[]{:T(128)}, u32[]{:S(2)}, u32[]{:S(2)}) collective-permute-start(f32[]{:T(128)} %get-tuple-element.21), channel_id=1, source_target_pairs={{0,1},{1,0},{2,3},{3,2},{4,5},{5,4},{6,7},{7,6},{8,9},{9,8},{10,11... | collective-permute-start | bytes 20 | tf_op jit(solution)/shard_map/ppermute | solution.py:14
  61.5 1.2 collective-permute-start.3
  64.7 1.2 collective-permute-start.4
  76.7 1.1 collective-permute-start.5
  84.5 1.4 collective-permute-start.6
  87.8 1.4 collective-permute-start.7
  91.1 1.4 collective-permute-start.8
  103.1 1.1 collective-permute-start.9
where the time goes:
time: 149 us; the launch traced here: 147 us
  local copies, waits for them, and re-layouts  46.2 us (31%)
  blocking collectives  35.7 us (24%)
  matrix products  24.7 us (17%)
  between operations  20.6 us (14%)
  other arithmetic  10.5 us (7%)
  waiting for transfers between devices  7.45 us (5%)
  starting transfers between devices  2.4 us (2%)
    psum x1, blocking collectives, per_device(): sweep_energy = lax.psum(contribution, 'seg')  35.7 us
    dot_general x3, matrix products, apply_operator(): jnp.einsum('nskil,nsklm->nsim', half_products, other_env, preferred_eleme...  23.8 us
    unnamed x6, local copies, waits for them, and re-layouts  15.5 us
    another operation x1, local copies, waits for them, and re-layouts  15.4 us
    slice x1, local copies, waits for them, and re-layouts, per_device(): own_env = environment[:, 0]  8.13 us
    ppermute x10, waiting for transfers between devices, swapped(): lax.ppermute(shard, axis, [(i, i ^ 1 << stride) for i in range(lax.axis_s...  7.45 us
  transfers between devices with their start and end apart: 10, of which 7 were waited for; matrix products, arithmetic and copies ran while one was open for 25% of the time, Pallas kernels for 0%

commit v1 on v0

v1 whole, which is shorter than its diff:
```python
import functools

import jax
import jax.numpy as jnp
from jax import lax
from jax.experimental import pallas as pl
from jax.experimental.pallas import tpu as pltpu
from jax.sharding import PartitionSpec as P

ITERS = 2
EPSILON = 1e-06
F32 = jnp.float32
BF16 = jnp.bfloat16


def ritz_pair(rayleigh, coupling, curvature):
    half_gap = 0.5 * (rayleigh - curvature)
    energy_now = 0.5 * (rayleigh + curvature) - jnp.sqrt(half_gap * half_gap + coupling * coupling)
    weight_old = curvature - energy_now
    weight_new = -coupling
    length_pair = jnp.sqrt(weight_old * weight_old + weight_new * weight_new)
    return energy_now, weight_old / length_pair, weight_new / length_pair


def project(vv, rayleigh, vc, cc, vh, ch, ci):
    squared = jnp.maximum(cc - vc * vc * (2.0 - vv), 0.0)
    inv = 1.0 / jnp.sqrt(squared + EPSILON)
    coupling = (vh - vc * rayleigh) * inv
    mirrored = (ci - vc * rayleigh) * inv
    curvature = (ch - vc * (ci + vh) + vc * vc * rayleigh) * (inv * inv)
    energy, old, new = ritz_pair(rayleigh, coupling, curvature)
    scale_c = new * inv
    scale_v = old - scale_c * vc
    next_rayleigh = old * old * rayleigh + old * new * (coupling + mirrored) + new * new * curvature
    next_vv = scale_v * scale_v * vv + 2.0 * scale_v * scale_c * vc + scale_c * scale_c * cc
    return energy, scale_v, scale_c, next_rayleigh, next_vv


def rows_of(*fields):
    rows = []
    for field in fields:
        if field.shape[0] > 1:
            field = jnp.sum(field, axis=0, keepdims=True)
        half = field.shape[1] // 128
        total = field[:, :128]
        for part in range(1, half):
            total = total + field[:, part * 128:(part + 1) * 128]
        rows.append(total)
    rows.append(jnp.zeros((8 - len(rows), 128), F32))
    stacked = jnp.concatenate(rows, axis=0)
    return jnp.broadcast_to(jnp.sum(stacked, axis=1, keepdims=True), (8, 128))


def kernel(
    n, chunk, psi_ref, sizes_ref, env_ref, wave_ref, energies_ref, sweep_ref,
    psi, own, other, parts, acc, diag_own, diag_other, stats, stats_in, gathered,
    psi_sem, own_sem, send_sem, recv_sem, stat_send, stat_recv, all_send, all_recv,
):
    channels, size = own.shape[0], own.shape[1]
    half = size // 2
    chunks = channels // chunk
    me = lax.axis_index("seg")
    parity = lax.rem(me, 2)
    partner = me + 1 - 2 * parity
    bond = lax.div(me, 2)
    odd = parity == 1

    barrier = pltpu.get_barrier_semaphore()
    for step in range(1, n):
        pl.semaphore_signal(
            barrier, inc=1, device_id={"seg": lax.rem(me + step, n)}, device_id_type=pl.DeviceIdType.MESH
        )
    psi_copy = pltpu.make_async_copy(psi_ref.at[0, 0], psi, psi_sem)
    psi_copy.start()
    own_copies = []
    for c in range(chunks):
        copy = pltpu.make_async_copy(
            env_ref.at[0, 0, 0, pl.ds(c * chunk, chunk)], own.at[pl.ds(c * chunk, chunk)], own_sem.at[c]
        )
        copy.start()
        own_copies.append(copy)
    pl.semaphore_wait(barrier, n - 1)

    def to_partner(src, dst, sent, received):
        copy = pltpu.make_async_remote_copy(
            src_ref=src, dst_ref=dst, send_sem=sent, recv_sem=received,
            device_id={"seg": partner}, device_id_type=pl.DeviceIdType.MESH,
        )
        copy.start()
        return copy

    sends = []
    for c in range(chunks):
        ks = pl.ds(c * chunk, chunk)
        sends.append((
            to_partner(
                env_ref.at[0, 1, 0, ks, pl.ds(0, half)], other.at[ks, pl.ds(0, half)],
                send_sem.at[2 * c], recv_sem.at[2 * c],
            ),
            to_partner(
                env_ref.at[0, 1, 0, ks, pl.ds(half, half), pl.ds(half, half)],
                other.at[ks, pl.ds(half, half), pl.ds(half, half)],
                send_sem.at[2 * c + 1], recv_sem.at[2 * c + 1],
            ),
        ))

    row_at = lax.broadcasted_iota(jnp.int32, (size, size), 0)
    col_at = lax.broadcasted_iota(jnp.int32, (size, size), 1)
    dim0, dim1 = sizes_ref[0, 0, 0], sizes_ref[0, 0, 1]
    row_size = jnp.where(odd, dim1, dim0)
    col_size = jnp.where(odd, dim0, dim1)

    def masked(field):
        return jnp.where((row_at < row_size) & (col_at < col_size), field, 0.0)

    def wide(row):
        return jnp.concatenate([row] * (size // 128), axis=1)

    eye = (
        lax.broadcasted_iota(jnp.int32, (half, half), 0) == lax.broadcasted_iota(jnp.int32, (half, half), 1)
    )

    def diagonals(ref, out, k):
        low = jnp.where(eye, ref[k, 0:half, 0:half].astype(F32), 0.0)
        high = jnp.where(eye, ref[k, half:size, half:size].astype(F32), 0.0)
        out[k:k + 1, 0:half] = jnp.sum(low, axis=0, keepdims=True)
        out[k:k + 1, half:size] = jnp.sum(high, axis=0, keepdims=True)

    diag_own[...] = jnp.zeros_like(diag_own)
    diag_other[...] = jnp.zeros_like(diag_other)

    psi_copy.wait()

    @pl.when(odd)
    def _():
        psi[...] = psi[...].T

    start = masked(psi[...])
    psi[...] = start
    lowered = start.astype(BF16)
    for c in range(chunks):
        own_copies[c].wait()
        for k in range(c * chunk, (c + 1) * chunk):
            parts[:, k * size:(k + 1) * size] = jnp.dot(
                own[k], lowered, preferred_element_type=F32
            ).astype(BF16)
            diagonals(own, diag_own, k)

    for c in range(chunks):
        for copy in sends[c]:
            copy.wait_recv()
        for k in range(c * chunk, (c + 1) * chunk):
            other[k, half:size, 0:half] = other[k, 0:half, half:size].T
            diagonals(other, diag_other, k)
        ks = slice(c * chunk * size, (c + 1) * chunk * size)
        product = jnp.dot(
            parts[:, ks],
            other[c * chunk:(c + 1) * chunk].reshape(chunk * size, size),
            preferred_element_type=F32,
        )
        acc[...] = product if c == 0 else acc[...] + product

    def apply_operator(field):
        low = field.astype(BF16)
        for k in range(channels):
            parts[:, k * size:(k + 1) * size] = jnp.dot(
                own[k], low, preferred_element_type=F32
            ).astype(BF16)
        return masked(jnp.dot(
            parts[...], other[...].reshape(channels * size, size), preferred_element_type=F32
        ))

    start = psi[...]
    image = masked(acc[...])
    stats[0] = rows_of(start * start, start * image)
    stat_copy = to_partner(stats.at[0], stats_in.at[0], stat_send.at[0], stat_recv.at[0])
    precondition = jnp.dot(
        diag_own[...].T.astype(BF16), diag_other[...].astype(BF16), preferred_element_type=F32
    )
    stat_copy.wait_recv()
    sends_left = [stat_copy]
    total = stats[0] + stats_in[0]
    squared = total[0:1] + EPSILON
    inv = 1.0 / jnp.sqrt(squared)
    rayleigh = total[1:2] / squared
    vv = total[0:1] / squared
    vector = start * wide(inv)
    image = image * wide(inv)

    def correction_of(vector, image, rayleigh):
        shift = wide(rayleigh)
        return (image - shift * vector) / jnp.maximum(jnp.abs(precondition - shift), 1.0)

    raw = correction_of(vector, image, rayleigh)
    raw_image = apply_operator(raw)
    stats[1] = rows_of(vector * raw, raw * raw, vector * raw_image, raw * raw_image, raw * image)
    stat_copy = to_partner(stats.at[1], stats_in.at[1], stat_send.at[1], stat_recv.at[1])
    stat_copy.wait_recv()
    sends_left.append(stat_copy)
    total = stats[1] + stats_in[1]
    energy_one, scale_v, scale_c, rayleigh, vv = project(
        vv, rayleigh, *(total[q:q + 1] for q in range(5))
    )
    vector = wide(scale_v) * vector + wide(scale_c) * raw
    image = wide(scale_v) * image + wide(scale_c) * raw_image

    raw = correction_of(vector, image, rayleigh)
    raw_image = apply_operator(raw)
    sums = rows_of(vector * raw, raw * raw, vector * raw_image, raw * raw_image, raw * image)
    share = 0.5
    gathered[parity, bond] = jnp.concatenate(
        [sums[0:5], share * vv, share * rayleigh, share * energy_one], axis=0
    )

    def to_device(target, slot):
        return pltpu.make_async_remote_copy(
            src_ref=gathered.at[parity, bond], dst_ref=gathered.at[parity, bond],
            send_sem=all_send.at[slot], recv_sem=all_recv.at[me],
            device_id={"seg": target}, device_id_type=pl.DeviceIdType.MESH,
        )

    def from_device(source):
        return pltpu.make_async_remote_copy(
            src_ref=gathered.at[parity, bond],
            dst_ref=gathered.at[lax.rem(source, 2), lax.div(source, 2)],
            send_sem=all_send.at[0], recv_sem=all_recv.at[source],
            device_id={"seg": source}, device_id_type=pl.DeviceIdType.MESH,
        )

    first = to_device(partner, 0)
    first.start()
    last_sends = [first]
    for step in range(1, n // 2):
        for side in range(2):
            copy = to_device(lax.rem(2 * bond + 2 * step + side, n), 2 * step - 1 + side)
            copy.start()
            last_sends.append(copy)
    from_device(partner).wait_recv()
    total = gathered[0, bond] + gathered[1, bond]
    energy_two, scale_v, scale_c, _, _ = project(
        total[5:6], total[6:7], *(total[q:q + 1] for q in range(5))
    )
    final = (wide(scale_v * float(size)) * vector + wide(scale_c * float(size)) * raw)

    @pl.when(odd)
    def _():
        wave_ref[0, 0] = final.T

    @pl.when(jnp.logical_not(odd))
    def _():
        wave_ref[0, 0] = final

    lane = lax.broadcasted_iota(jnp.int32, (1, 128), 1)
    energies_ref[...] = jnp.where(lane == 0, total[7:8], energy_two)[:, 0:ITERS]

    for step in range(1, n // 2):
        for side in range(2):
            from_device(lax.rem(2 * bond + 2 * step + side, n)).wait_recv()
    bonds = n // 2
    sums = [gathered[0, :, q, :] + gathered[1, :, q, :] for q in range(8)]
    bond_energy, _, _, _, _ = project(sums[5], sums[6], *sums[0:5])
    place = lax.broadcasted_iota(jnp.int32, (bonds, 128), 0).astype(F32)
    weight = (1.0 + 2.0 * place / float(max(bonds - 1, 1))) / float(bonds)
    sweep_one = jnp.sum(weight * sums[7], axis=0, keepdims=True)
    sweep_two = jnp.sum(weight * bond_energy, axis=0, keepdims=True)
    sweep_ref[0] = sweep_one[0, 0]
    sweep_ref[1] = sweep_two[0, 0]

    for copy in sends_left + last_sends:
        copy.wait_send()
    for pair in sends:
        for copy in pair:
            copy.wait_send()


def per_device(n, psi_start, block_sizes, environment):
    channels, size = environment.shape[3], environment.shape[4]
    chunk = 2 if channels % 2 == 0 else 1
    chunks = channels // chunk
    padded = -(-channels // 16) * 16
    bonds = n // 2
    dma = pltpu.SemaphoreType.DMA
    return pl.pallas_call(
        functools.partial(kernel, n, chunk),
        out_shape=(
            jax.ShapeDtypeStruct(psi_start.shape, F32),
            jax.ShapeDtypeStruct((1, ITERS), F32),
            jax.ShapeDtypeStruct((ITERS,), F32),
        ),
        in_specs=[
            pl.BlockSpec(memory_space=pl.ANY),
            pl.BlockSpec(memory_space=pltpu.SMEM),
            pl.BlockSpec(memory_space=pl.ANY),
        ],
        out_specs=(
            pl.BlockSpec(memory_space=pltpu.VMEM),
            pl.BlockSpec(memory_space=pltpu.VMEM),
            pl.BlockSpec(memory_space=pltpu.SMEM),
        ),
        scratch_shapes=[
            pltpu.VMEM((size, size), F32),
            pltpu.VMEM((channels, size, size), BF16),
            pltpu.VMEM((channels, size, size), BF16),
            pltpu.VMEM((size, channels * size), BF16),
            pltpu.VMEM((size, size), F32),
            pltpu.VMEM((padded, size), F32),
            pltpu.VMEM((padded, size), F32),
            pltpu.VMEM((2, 8, 128), F32),
            pltpu.VMEM((2, 8, 128), F32),
            pltpu.VMEM((2, bonds, 8, 128), F32),
            dma,
            dma((chunks,)),
            dma((2 * chunks,)),
            dma((2 * chunks,)),
            dma((2,)),
            dma((2,)),
            dma((n,)),
            dma((n,)),
        ],
        compiler_params=pltpu.CompilerParams(
            collective_id=0, has_side_effects=True, vmem_limit_bytes=48 * 1024 * 1024
        ),
    )(psi_start, block_sizes, environment)


def solution(mesh):
    in_specs = (
        P(("groups", "seg"), None, None, None),
        P(("groups", "seg"), None, None),
        P(("groups", "seg"), None, None, None, None, None),
    )
    out_specs = (P(("groups", "seg"), None, None, None), P(("groups", "seg"), None), P("groups"))
    return jax.shard_map(
        functools.partial(per_device, mesh.shape["seg"]),
        mesh=mesh, in_specs=in_specs, out_specs=out_specs, check_vma=False,
    )
```

time: 149 us -> 34 us (0.23)
  local copies, waits for them, and re-layouts: 46.2 us -> 3.32 us
  blocking collectives: 35.7 us -> 0 us
  Pallas kernels: 0 us -> 29.8 us
  matrix products: 24.7 us -> 0 us
  between operations: 20.6 us -> 0.65 us
  other arithmetic: 10.5 us -> 0 us
  waiting for transfers between devices: 7.45 us -> 0 us
  starting transfers between devices: 2.4 us -> 0 us
    psum x1 -> x0, blocking collectives: 35.7 us -> none  [per_device(): sweep_energy = lax.psum(contribution, 'seg')]
    pallas_call x0 -> x1, Pallas kernels: none -> 29.8 us  [per_device(): pl.pallas_call(functools.partial(kernel, n, chunk), out_shape=(jax.ShapeD...]
    dot_general x4 -> x0, matrix products: 24.7 us -> none  [the longest x3 23.8 us: apply_operator(): jnp.einsum('nskil,nsklm->nsim', half_products, other_env, preferred_eleme...]
    another operation x1 -> x0, local copies, waits for them, and re-layouts: 15.4 us -> none
    unnamed x6 -> x7, local copies, waits for them, and re-layouts: 15.5 us -> 3.32 us
    slice x4 -> x0, local copies, waits for them, and re-layouts: 9.88 us -> none  [the longest x1 8.13 us: per_device(): own_env = environment[:, 0]]
    ppermute x10 -> x0, waiting for transfers between devices: 7.45 us -> none  [swapped(): lax.ppermute(shard, axis, [(i, i ^ 1 << stride) for i in range(lax.axis_s...]
    gather x2 -> x0, local copies, waits for them, and re-layouts: 5.3 us -> none  [the longest x1 2.65 us: diagonal_terms(): own_diag = jnp.diagonal(own_env, axis1=-2, axis2=-1).astype(jnp.float32)]
  transfers between devices with their start and end apart: 10 -> 0, of which waited for: 7 -> 0; matrix products, arithmetic and copies ran while one was open for 25% -> 0% of each run, Pallas kernels for 0% -> 0%
where the time goes in v1:
time: 34 us; the launch traced here: 33.8 us
  Pallas kernels  29.8 us (88%)
  local copies, waits for them, and re-layouts  3.32 us (10%)
  between operations  0.65 us (2%)
    pallas_call x1, Pallas kernels, per_device(): pl.pallas_call(functools.partial(kernel, n, chunk), out_shape=(jax.ShapeD...  29.8 us
    unnamed x7, local copies, waits for them, and re-layouts  3.32 us

profile of v1, /device:TPU:0, one launch (start us, length us, event | category | flops | bytes accessed | tf_op | source)
XLA Modules:
  0.0 33.8 jit_solution(14191930260994987926)
XLA Ops:
  0.6 0.0 copy-start
  0.6 0.9 %copy-done = f32[1,1,256,256]{3,2,1,0:T(8,128)S(1)} copy-done((f32[1,1,256,256]{3,2,1,0:T(8,128)S(1)}, f32[1,1,256,256]{3,2,1,0:T(8,128)}, u32[]{:S(2)}) %copy-start) | copy-done | bytes 262168
  1.6 0.0 copy-start.1
  1.6 0.7 %copy-done.1 = s32[1,1,2]{2,1,0:T(1,128)S(1)} copy-done((s32[1,1,2]{2,1,0:T(1,128)S(1)}, s32[1,1,2]{2,1,0:T(1,128)}, u32[]{:S(2)}) %copy-start.1) | copy-done | bytes 32
  2.2 29.8 %shard_map.58 = (f32[1,1,256,256]{3,2,1,0:T(8,128)S(1)}, f32[1,2]{1,0:T(1,128)S(1)}, f32[2]{0:T(128)S(1)}) custom-call(f32[1,1,256,256]{3,2,1,0:T(8,128)S(1)} %copy-done, s32[1,1,2]{2,1,0:T(1,128)S(1)} %copy-done.1, bf16[1,2,1,34,256,256]{5,4,3,2,1,0:T(8,128)(2,1)} %env_ref.1), custom_call_target="tpu_custom_call" | custom-call | tf_op jit(solution)/shard_map/pallas_call | solution.py:283
  32.1 0.7 %copy.9 = f32[1,1,256,256]{3,2,1,0:T(8,128)} copy(f32[1,1,256,256]{3,2,1,0:T(8,128)S(1)} %get-tuple-element.6) | data formatting | bytes 524288
  32.8 0.5 %copy.10 = f32[1,2]{1,0:T(1,128)} copy(f32[1,2]{1,0:T(1,128)S(1)} %get-tuple-element.7) | data formatting | bytes 16
  33.3 0.5 %copy.11 = f32[2]{0:T(128)} copy(f32[2]{0:T(128)S(1)} %get-tuple-element.8) | data formatting | bytes 16
Async XLA Ops:
  0.6 1.0 %copy-start = (f32[1,1,256,256]{3,2,1,0:T(8,128)S(1)}, f32[1,1,256,256]{3,2,1,0:T(8,128)}, u32[]{:S(2)}) copy-start(f32[1,1,256,256]{3,2,1,0:T(8,128)} %psi_ref.1) | copy-start | bytes 786436
  1.6 0.7 %copy-start.1 = (s32[1,1,2]{2,1,0:T(1,128)S(1)}, s32[1,1,2]{2,1,0:T(1,128)}, u32[]{:S(2)}) copy-start(s32[1,1,2]{2,1,0:T(1,128)} %sizes_ref.1) | copy-start | bytes 28

commit v2 on v1

--- a/solution.py
+++ b/solution.py
@@ -8,6 +8,7 @@
 from jax.sharding import PartitionSpec as P
 
 ITERS = 2
+MARKS = (0, 10, 20, 28, 34)
 EPSILON = 1e-06
 F32 = jnp.float32
 BF16 = jnp.bfloat16
@@ -52,13 +53,12 @@
 
 
 def kernel(
-    n, chunk, psi_ref, sizes_ref, env_ref, wave_ref, energies_ref, sweep_ref,
-    psi, own, other, parts, acc, diag_own, diag_other, stats, stats_in, gathered,
+    n, groups, psi_ref, sizes_ref, env_ref, wave_ref, energies_ref, sweep_ref,
+    psi, own, other, parts, diag_own, diag_other, stats, stats_in, gathered,
     psi_sem, own_sem, send_sem, recv_sem, stat_send, stat_recv, all_send, all_recv,
 ):
     channels, size = own.shape[0], own.shape[1]
     half = size // 2
-    chunks = channels // chunk
     me = lax.axis_index("seg")
     parity = lax.rem(me, 2)
     partner = me + 1 - 2 * parity
@@ -73,13 +73,10 @@
     psi_copy = pltpu.make_async_copy(psi_ref.at[0, 0], psi, psi_sem)
     psi_copy.start()
     own_copies = []
-    for c in range(chunks):
-        copy = pltpu.make_async_copy(
-            env_ref.at[0, 0, 0, pl.ds(c * chunk, chunk)], own.at[pl.ds(c * chunk, chunk)], own_sem.at[c]
-        )
-        copy.start()
-        own_copies.append(copy)
-    pl.semaphore_wait(barrier, n - 1)
+    for g, (low, high) in enumerate(groups):
+        ks = pl.ds(low, high - low)
+        own_copies.append(pltpu.make_async_copy(env_ref.at[0, 0, 0, ks], own.at[ks], own_sem.at[g]))
+        own_copies[-1].start()
 
     def to_partner(src, dst, sent, received):
         copy = pltpu.make_async_remote_copy(
@@ -89,20 +86,13 @@
         copy.start()
         return copy
 
-    sends = []
-    for c in range(chunks):
-        ks = pl.ds(c * chunk, chunk)
-        sends.append((
-            to_partner(
-                env_ref.at[0, 1, 0, ks, pl.ds(0, half)], other.at[ks, pl.ds(0, half)],
-                send_sem.at[2 * c], recv_sem.at[2 * c],
-            ),
-            to_partner(
-                env_ref.at[0, 1, 0, ks, pl.ds(half, half), pl.ds(half, half)],
-                other.at[ks, pl.ds(half, half), pl.ds(half, half)],
-                send_sem.at[2 * c + 1], recv_sem.at[2 * c + 1],
-            ),
-        ))
+    stat_copies = []
+
+    def exchange(slot, sums):
+        stats[slot] = sums
+        copy = to_partner(stats.at[slot], stats_in.at[slot], stat_send.at[slot], stat_recv.at[slot])
+        stat_copies.append(copy)
+        return copy
 
     row_at = lax.broadcasted_iota(jnp.int32, (size, size), 0)
     col_at = lax.broadcasted_iota(jnp.int32, (size, size), 1)
@@ -126,8 +116,19 @@
         out[k:k + 1, 0:half] = jnp.sum(low, axis=0, keepdims=True)
         out[k:k + 1, half:size] = jnp.sum(high, axis=0, keepdims=True)
 
-    diag_own[...] = jnp.zeros_like(diag_own)
-    diag_other[...] = jnp.zeros_like(diag_other)
+    def stage_one(low, first, last):
+        products = jnp.dot(
+            own[first:last].reshape((last - first) * size, size), low, preferred_element_type=F32
+        ).astype(BF16)
+        for k in range(first, last):
+            parts[:, k * size:(k + 1) * size] = products[(k - first) * size:(k - first + 1) * size]
+
+    def stage_two(first, last):
+        return jnp.dot(
+            parts[:, first * size:last * size],
+            other[first:last].reshape((last - first) * size, size),
+            preferred_element_type=F32,
+        )
 
     psi_copy.wait()
 
@@ -137,55 +138,60 @@
 
     start = masked(psi[...])
     psi[...] = start
-    lowered = start.astype(BF16)
-    for c in range(chunks):
-        own_copies[c].wait()
-        for k in range(c * chunk, (c + 1) * chunk):
-            parts[:, k * size:(k + 1) * size] = jnp.dot(
-                own[k], lowered, preferred_element_type=F32
-            ).astype(BF16)
-            diagonals(own, diag_own, k)
-
-    for c in range(chunks):
-        for copy in sends[c]:
+    sums = rows_of(start * start)
+    pl.semaphore_wait(barrier, n - 1)
+
+    norm_copy = exchange(0, sums)
+    sends = []
+    for g, (low, high) in enumerate(groups):
+        ks = pl.ds(low, high - low)
+        sends.append((
+            to_partner(
+                env_ref.at[0, 1, 0, ks, pl.ds(0, half)], other.at[ks, pl.ds(0, half)],
+                send_sem.at[0, g], recv_sem.at[0, g],
+            ),
+            to_partner(
+                env_ref.at[0, 1, 0, ks, pl.ds(half, half), pl.ds(half, half)],
+                other.at[ks, pl.ds(half, half), pl.ds(half, half)],
+                send_sem.at[1, g], recv_sem.at[1, g],
+            ),
+        ))
+    diag_own[...] = jnp.zeros_like(diag_own)
+    diag_other[...] = jnp.zeros_like(diag_other)
+    for copy in own_copies:
+        copy.wait()
+    norm_copy.wait_recv()
+    total = stats[0] + stats_in[0]
+    squared = total[0:1] + EPSILON
+    vv = total[0:1] / squared
+    psi[...] = psi[...] * wide(1.0 / jnp.sqrt(squared))
+    stage_one(psi[...].astype(BF16), 0, channels)
+    for k in range(channels):
+        diagonals(own, diag_own, k)
+
+    image = None
+    for (low, high), copies in zip(groups, sends):
+        for copy in copies:
             copy.wait_recv()
-        for k in range(c * chunk, (c + 1) * chunk):
+        for k in range(low, high):
             other[k, half:size, 0:half] = other[k, 0:half, half:size].T
-            diagonals(other, diag_other, k)
-        ks = slice(c * chunk * size, (c + 1) * chunk * size)
-        product = jnp.dot(
-            parts[:, ks],
-            other[c * chunk:(c + 1) * chunk].reshape(chunk * size, size),
-            preferred_element_type=F32,
-        )
-        acc[...] = product if c == 0 else acc[...] + product
+        product = stage_two(low, high)
+        image = product if image is None else image + product
 
     def apply_operator(field):
-        low = field.astype(BF16)
-        for k in range(channels):
-            parts[:, k * size:(k + 1) * size] = jnp.dot(
-                own[k], low, preferred_element_type=F32
-            ).astype(BF16)
-        return masked(jnp.dot(
-            parts[...], other[...].reshape(channels * size, size), preferred_element_type=F32
-        ))
-
-    start = psi[...]
-    image = masked(acc[...])
-    stats[0] = rows_of(start * start, start * image)
-    stat_copy = to_partner(stats.at[0], stats_in.at[0], stat_send.at[0], stat_recv.at[0])
+        stage_one(field.astype(BF16), 0, channels)
+        return masked(stage_two(0, channels))
+
+    vector = psi[...]
+    image = masked(image)
+    rayleigh_copy = exchange(1, rows_of(vector * image))
+    for k in range(channels):
+        diagonals(other, diag_other, k)
     precondition = jnp.dot(
         diag_own[...].T.astype(BF16), diag_other[...].astype(BF16), preferred_element_type=F32
     )
-    stat_copy.wait_recv()
-    sends_left = [stat_copy]
-    total = stats[0] + stats_in[0]
-    squared = total[0:1] + EPSILON
-    inv = 1.0 / jnp.sqrt(squared)
-    rayleigh = total[1:2] / squared
-    vv = total[0:1] / squared
-    vector = start * wide(inv)
-    image = image * wide(inv)
+    rayleigh_copy.wait_recv()
+    rayleigh = stats[1, 0:1] + stats_in[1, 0:1]
 
     def correction_of(vector, image, rayleigh):
         shift = wide(rayleigh)
@@ -193,11 +199,10 @@
 
     raw = correction_of(vector, image, rayleigh)
     raw_image = apply_operator(raw)
-    stats[1] = rows_of(vector * raw, raw * raw, vector * raw_image, raw * raw_image, raw * image)
-    stat_copy = to_partner(stats.at[1], stats_in.at[1], stat_send.at[1], stat_recv.at[1])
-    stat_copy.wait_recv()
-    sends_left.append(stat_copy)
-    total = stats[1] + stats_in[1]
+    exchange(
+        2, rows_of(vector * raw, raw * raw, vector * raw_image, raw * raw_image, raw * image)
+    ).wait_recv()
+    total = stats[2] + stats_in[2]
     energy_one, scale_v, scale_c, rayleigh, vv = project(
         vv, rayleigh, *(total[q:q + 1] for q in range(5))
     )
@@ -227,10 +232,11 @@
             device_id={"seg": source}, device_id_type=pl.DeviceIdType.MESH,
         )
 
+    far_first = sorted(range(1, n // 2), key=lambda step: abs(step - n // 4))
     first = to_device(partner, 0)
     first.start()
     last_sends = [first]
-    for step in range(1, n // 2):
+    for step in far_first:
         for side in range(2):
             copy = to_device(lax.rem(2 * bond + 2 * step + side, n), 2 * step - 1 + side)
             copy.start()
@@ -266,22 +272,27 @@
     sweep_ref[0] = sweep_one[0, 0]
     sweep_ref[1] = sweep_two[0, 0]
 
-    for copy in sends_left + last_sends:
+    for copy in stat_copies + last_sends:
         copy.wait_send()
     for pair in sends:
         for copy in pair:
             copy.wait_send()
 
 
+def group_bounds(channels):
+    marks = sorted({channels * m // 34 for m in MARKS})
+    return list(zip(marks[:-1], marks[1:]))
+
+
 def per_device(n, psi_start, block_sizes, environment):
     channels, size = environment.shape[3], environment.shape[4]
-    chunk = 2 if channels % 2 == 0 else 1
-    chunks = channels // chunk
+    groups = group_bounds(channels)
+    chunks = len(groups)
     padded = -(-channels // 16) * 16
     bonds = n // 2
     dma = pltpu.SemaphoreType.DMA
     return pl.pallas_call(
-        functools.partial(kernel, n, chunk),
+        functools.partial(kernel, n, groups),
         out_shape=(
             jax.ShapeDtypeStruct(psi_start.shape, F32),
             jax.ShapeDtypeStruct((1, ITERS), F32),
@@ -302,18 +313,17 @@
             pltpu.VMEM((channels, size, size), BF16),
             pltpu.VMEM((channels, size, size), BF16),
             pltpu.VMEM((size, channels * size), BF16),
-            pltpu.VMEM((size, size), F32),
             pltpu.VMEM((padded, size), F32),
             pltpu.VMEM((padded, size), F32),
-            pltpu.VMEM((2, 8, 128), F32),
-            pltpu.VMEM((2, 8, 128), F32),
+            pltpu.VMEM((3, 8, 128), F32),
+            pltpu.VMEM((3, 8, 128), F32),
             pltpu.VMEM((2, bonds, 8, 128), F32),
             dma,
             dma((chunks,)),
-            dma((2 * chunks,)),
-            dma((2 * chunks,)),
-            dma((2,)),
-            dma((2,)),
+            dma((2, chunks)),
+            dma((2, chunks)),
+            dma((3,)),
+            dma((3,)),
             dma((n,)),
             dma((n,)),
         ],

time: 34 us -> 29.7 us (0.87)
  Pallas kernels: 29.8 us -> 25.6 us
    pallas_call x1, Pallas kernels: 29.8 us -> 25.6 us  [per_device(): pl.pallas_call(functools.partial(kernel, n, groups), out_shape=(jax.Shape...]
where the time goes in v2:
time: 29.7 us; the launch traced here: 29.5 us
  Pallas kernels  25.6 us (86%)
  local copies, waits for them, and re-layouts  3.32 us (11%)
  between operations  0.65 us (2%)
    pallas_call x1, Pallas kernels, per_device(): pl.pallas_call(functools.partial(kernel, n, groups), out_shape=(jax.Shape...  25.6 us
    unnamed x7, local copies, waits for them, and re-layouts  3.32 us

profile of v2, /device:TPU:0, one launch (start us, length us, event | category | flops | bytes accessed | tf_op | source)
XLA Modules:
  0.0 29.5 jit_solution(6100271784491803483)
XLA Ops:
  0.6 0.0 copy-start
  0.6 0.9 %copy-done = f32[1,1,256,256]{3,2,1,0:T(8,128)S(1)} copy-done((f32[1,1,256,256]{3,2,1,0:T(8,128)S(1)}, f32[1,1,256,256]{3,2,1,0:T(8,128)}, u32[]{:S(2)}) %copy-start) | copy-done | bytes 262168
  1.6 0.0 copy-start.1
  1.6 0.7 %copy-done.1 = s32[1,1,2]{2,1,0:T(1,128)S(1)} copy-done((s32[1,1,2]{2,1,0:T(1,128)S(1)}, s32[1,1,2]{2,1,0:T(1,128)}, u32[]{:S(2)}) %copy-start.1) | copy-done | bytes 32
  2.2 25.6 %shard_map.58 = (f32[1,1,256,256]{3,2,1,0:T(8,128)S(1)}, f32[1,2]{1,0:T(1,128)S(1)}, f32[2]{0:T(128)S(1)}) custom-call(f32[1,1,256,256]{3,2,1,0:T(8,128)S(1)} %copy-done, s32[1,1,2]{2,1,0:T(1,128)S(1)} %copy-done.1, bf16[1,2,1,34,256,256]{5,4,3,2,1,0:T(8,128)(2,1)} %env_ref.1), custom_call_target="tpu_custom_call" | custom-call | tf_op jit(solution)/shard_map/pallas_call | solution.py:294
  27.8 0.7 %copy.9 = f32[1,1,256,256]{3,2,1,0:T(8,128)} copy(f32[1,1,256,256]{3,2,1,0:T(8,128)S(1)} %get-tuple-element.6) | data formatting | bytes 524288
  28.5 0.5 %copy.10 = f32[1,2]{1,0:T(1,128)} copy(f32[1,2]{1,0:T(1,128)S(1)} %get-tuple-element.7) | data formatting | bytes 16
  29.0 0.5 %copy.11 = f32[2]{0:T(128)} copy(f32[2]{0:T(128)S(1)} %get-tuple-element.8) | data formatting | bytes 16
Async XLA Ops:
  0.6 1.0 %copy-start = (f32[1,1,256,256]{3,2,1,0:T(8,128)S(1)}, f32[1,1,256,256]{3,2,1,0:T(8,128)}, u32[]{:S(2)}) copy-start(f32[1,1,256,256]{3,2,1,0:T(8,128)} %psi_ref.1) | copy-start | bytes 786436
  1.6 0.7 %copy-start.1 = (s32[1,1,2]{2,1,0:T(1,128)S(1)}, s32[1,1,2]{2,1,0:T(1,128)}, u32[]{:S(2)}) copy-start(s32[1,1,2]{2,1,0:T(1,128)} %sizes_ref.1) | copy-start | bytes 28

commit v3 on v2

--- a/solution.py
+++ b/solution.py
@@ -250,12 +250,14 @@
 
     @pl.when(odd)
     def _():
-        wave_ref[0, 0] = final.T
+        psi[...] = final.T
 
     @pl.when(jnp.logical_not(odd))
     def _():
-        wave_ref[0, 0] = final
-
+        psi[...] = final
+
+    wave_copy = pltpu.make_async_copy(psi, wave_ref.at[0, 0], psi_sem)
+    wave_copy.start()
     lane = lax.broadcasted_iota(jnp.int32, (1, 128), 1)
     energies_ref[...] = jnp.where(lane == 0, total[7:8], energy_two)[:, 0:ITERS]
 
@@ -272,6 +274,7 @@
     sweep_ref[0] = sweep_one[0, 0]
     sweep_ref[1] = sweep_two[0, 0]
 
+    wave_copy.wait()
     for copy in stat_copies + last_sends:
         copy.wait_send()
     for pair in sends:
@@ -291,7 +294,7 @@
     padded = -(-channels // 16) * 16
     bonds = n // 2
     dma = pltpu.SemaphoreType.DMA
-    return pl.pallas_call(
+    results = pl.pallas_call(
         functools.partial(kernel, n, groups),
         out_shape=(
             jax.ShapeDtypeStruct(psi_start.shape, F32),
@@ -304,7 +307,7 @@
             pl.BlockSpec(memory_space=pl.ANY),
         ],
         out_specs=(
-            pl.BlockSpec(memory_space=pltpu.VMEM),
+            pl.BlockSpec(memory_space=pl.ANY),
             pl.BlockSpec(memory_space=pltpu.VMEM),
             pl.BlockSpec(memory_space=pltpu.SMEM),
         ),
@@ -328,9 +331,21 @@
             dma((n,)),
         ],
         compiler_params=pltpu.CompilerParams(
-            collective_id=0, has_side_effects=True, vmem_limit_bytes=48 * 1024 * 1024
+            collective_id=0, has_side_effects=True, vmem_limit_bytes=60 * 1024 * 1024
         ),
     )(psi_start, block_sizes, environment)
+    return pl.pallas_call(
+        hand_over,
+        out_shape=tuple(jax.ShapeDtypeStruct(r.shape, r.dtype) for r in results),
+        in_specs=[pl.BlockSpec(memory_space=pltpu.VMEM)] * 3,
+        out_specs=tuple([pl.BlockSpec(memory_space=pltpu.VMEM)] * 3),
+    )(*results)
+
+
+def hand_over(wave, energies, sweep, wave_out, energies_out, sweep_out):
+    wave_out[...] = wave[...]
+    energies_out[...] = energies[...]
+    sweep_out[...] = sweep[...]
 
 
 def solution(mesh):

time: 29.7 us -> 29.1 us (0.980)
  local copies, waits for them, and re-layouts: 3.32 us -> 0 us
  Pallas kernels: 25.6 us -> 28.3 us
    unnamed x7 -> x0, local copies, waits for them, and re-layouts: 3.32 us -> none
    pallas_call x0 -> x1, Pallas kernels: none -> 1.68 us  [per_device(): pl.pallas_call(hand_over, out_shape=tuple((jax.ShapeDtypeStruct(r.shape,...]
    pallas_call x1, Pallas kernels: 25.6 us -> 26.6 us  [per_device(): pl.pallas_call(functools.partial(kernel, n, groups), out_shape=(jax.Shape...]
where the time goes in v3:
time: 29.1 us; the launch traced here: 28.9 us
  Pallas kernels  28.3 us (97%)
  between operations  0.64 us (2%)
    pallas_call x1, Pallas kernels, per_device(): pl.pallas_call(functools.partial(kernel, n, groups), out_shape=(jax.Shape...  26.6 us
    pallas_call x1, Pallas kernels, per_device(): pl.pallas_call(hand_over, out_shape=tuple((jax.ShapeDtypeStruct(r.shape,...  1.68 us

profile of v3, /device:TPU:0, one launch (start us, length us, event | category | flops | bytes accessed | tf_op | source)
XLA Modules:
  0.0 28.9 jit_solution(8717744757241114584)
XLA Ops:
  0.6 26.6 %shard_map.58 = (f32[1,1,256,256]{3,2,1,0:T(8,128)}, f32[1,2]{1,0:T(1,128)}, f32[2]{0:T(128)}) custom-call(f32[1,1,256,256]{3,2,1,0:T(8,128)} %psi_ref.1, s32[1,1,2]{2,1,0:T(1,128)} %sizes_ref.1, bf16[1,2,1,34,256,256]{5,4,3,2,1,0:T(8,128)(2,1)} %env_ref.1), custom_call_target="tpu_custom_call" | custom-call | tf_op jit(solution)/shard_map/pallas_call | solution.py:297
  27.2 1.7 %shard_map.59 = (f32[1,1,256,256]{3,2,1,0:T(8,128)}, f32[1,2]{1,0:T(1,128)}, f32[2]{0:T(128)}) custom-call(f32[1,1,256,256]{3,2,1,0:T(8,128)} %get-tuple-element.6.wave, f32[1,2]{1,0:T(1,128)} %get-tuple-element.7.energies, f32[2]{0:T(128)} %get-tuple-element.8.sweep), custom_call_target="tpu_custom_call" | custom-call | tf_op jit(solution)/shard_map/pallas_call | solution.py:337

commit v4 on v3

--- a/solution.py
+++ b/solution.py
@@ -166,9 +166,6 @@
     vv = total[0:1] / squared
     psi[...] = psi[...] * wide(1.0 / jnp.sqrt(squared))
     stage_one(psi[...].astype(BF16), 0, channels)
-    for k in range(channels):
-        diagonals(own, diag_own, k)
-
     image = None
     for (low, high), copies in zip(groups, sends):
         for copy in copies:
@@ -179,13 +176,19 @@
         image = product if image is None else image + product
 
     def apply_operator(field):
-        stage_one(field.astype(BF16), 0, channels)
-        return masked(stage_two(0, channels))
+        products = jnp.dot(
+            own[...].reshape(channels * size, size), field.astype(BF16), preferred_element_type=F32
+        ).astype(BF16)
+        joined = jnp.concatenate([products[k * size:(k + 1) * size] for k in range(channels)], axis=1)
+        return masked(jnp.dot(
+            joined, other[...].reshape(channels * size, size), preferred_element_type=F32
+        ))
 
     vector = psi[...]
     image = masked(image)
     rayleigh_copy = exchange(1, rows_of(vector * image))
     for k in range(channels):
+        diagonals(own, diag_own, k)
         diagonals(other, diag_other, k)
     precondition = jnp.dot(
         diag_own[...].T.astype(BF16), diag_other[...].astype(BF16), preferred_element_type=F32

time: 29.1 us -> 29.1 us (level)
  no operation moved by 1% of the time
where the time goes in v4:
time: 29.1 us; the launch traced here: 29 us
  Pallas kernels  28.3 us (97%)
  between operations  0.64 us (2%)
    pallas_call x1, Pallas kernels, per_device(): pl.pallas_call(functools.partial(kernel, n, groups), out_shape=(jax.Shape...  26.7 us
    pallas_call x1, Pallas kernels, per_device(): pl.pallas_call(hand_over, out_shape=tuple((jax.ShapeDtypeStruct(r.shape,...  1.68 us

profile of v4, /device:TPU:0, one launch (start us, length us, event | category | flops | bytes accessed | tf_op | source)
XLA Modules:
  0.0 29.0 jit_solution(16343856381969366224)
XLA Ops:
  0.6 26.7 %shard_map.58 = (f32[1,1,256,256]{3,2,1,0:T(8,128)}, f32[1,2]{1,0:T(1,128)}, f32[2]{0:T(128)}) custom-call(f32[1,1,256,256]{3,2,1,0:T(8,128)} %psi_ref.1, s32[1,1,2]{2,1,0:T(1,128)} %sizes_ref.1, bf16[1,2,1,34,256,256]{5,4,3,2,1,0:T(8,128)(2,1)} %env_ref.1), custom_call_target="tpu_custom_call" | custom-call | tf_op jit(solution)/shard_map/pallas_call | solution.py:300
  27.3 1.7 %shard_map.59 = (f32[1,1,256,256]{3,2,1,0:T(8,128)}, f32[1,2]{1,0:T(1,128)}, f32[2]{0:T(128)}) custom-call(f32[1,1,256,256]{3,2,1,0:T(8,128)} %get-tuple-element.6.wave, f32[1,2]{1,0:T(1,128)} %get-tuple-element.7.energies, f32[2]{0:T(128)} %get-tuple-element.8.sweep), custom_call_target="tpu_custom_call" | custom-call | tf_op jit(solution)/shard_map/pallas_call | solution.py:340
